TPU v7x, 128 devices: a whole 4x4x4 slice. The times are simulated.
128 devices in a mesh: sec: 2 (over y_lo), dev: 64 (over y_hi, x, z, core).
Axes of the slice: x: 4, y: 4 (y_hi: 2, y_lo: 2; y = y_hi * 2 + y_lo), z: 4, core: 2. Of those that a mesh axis runs over, the one named last changes fastest.
Arguments:
- flow_state: float32 [5, 8, 4096, 512], P(None, None, ('sec', 'dev')), may hold values from -6 to 6
- diffusion: float32 [8, 4096, 512], P(None, ('sec', 'dev')), may hold values from 0.02 to 0.1
- wall_stress: float32 [2, 4096, 512], P(None, ('sec', 'dev')), may hold values from -3 to 3
- batch_counts: int32 [128, 192], P(('sec', 'dev')), may hold values from 1 to 4, 480 in all within a row
- batch_routes: int32 [24576, 1], P(('sec', 'dev')), may hold values from 0 to 127; in each aligned block of 192 rows (0 to 191, 192 to 383, ...) at most 2 rows name the same one
- wall_index: int32 [24576, 4], P(('sec', 'dev')), may hold values from 0 to 16383, as said below
- input_weight: bfloat16 [12, 2048], replicated, may hold values from -1.75 to 1.75
- middle_weight: bfloat16 [2048, 2048], P(('sec', 'dev')), may hold values from -0.125 to 0.125
- output_weight: bfloat16 [2, 2048], replicated, may hold values from -0.125 to 0.125
Outputs:
- new_field: float32 [5, 8, 4096, 512], P(None, None, ('sec', 'dev'))
- new_stress: float32 [2, 4096, 512], P(None, ('sec', 'dev'))
- batch_loss: float32 [128], P(('sec', 'dev'))
- grad_w_in: float32 [12, 2048], replicated
- grad_w_mid: float32 [2048, 2048], P(('sec', 'dev'))
Inputs may be any that keep to these rules, and one draw needn't show every extreme that they name: `batch_routes`: within the 192 rows of one device no trainer is named more than 2 times, and every trainer is named by some row. `batch_counts`: each device's row sums to 480. `wall_index`: all entries of the 192 rows of one device are distinct.
All inputs are finite; a program needn't handle non-finite values.
Results may differ from a plain program's by a relative error of at most 0.00091.
Values may be sent and summed in bfloat16 or wider, within the bound.
A program may use at most 128 MiB of HBM per device.

v0:
```python
import math

import jax
import jax.numpy as jnp
from jax import lax
from jax.sharding import PartitionSpec as P

SLOTS = 2


advect_number = 0.3
wall_gain = 0.5
grad_number = 32.0


def extended(block, sides, width):
    for axis, dim in sides:
        count = lax.axis_size(axis)
        forward = [(i, i + 1) for i in range(count - 1)]
        forward.append((count - 1, 0))
        backward = [(target, source) for source, target in forward]
        low = lax.ppermute(
            lax.slice_in_dim(block, block.shape[dim] - width, None, axis=dim), axis, forward
        )
        high = lax.ppermute(lax.slice_in_dim(block, 0, width, axis=dim), axis, backward)
        block = jnp.concatenate([low, block, high], axis=dim)
    return block


def advance(flow_state, diffusion, below_z, above_z):
    below_x = jnp.concatenate([flow_state[..., :1], flow_state[..., :-1]], axis=3)
    above_x = jnp.concatenate([flow_state[..., 1:], flow_state[..., -1:]], axis=3)
    below_y = jnp.concatenate([flow_state[:, :1], flow_state[:, :-1]], axis=1)
    above_y = jnp.concatenate([flow_state[:, 1:], flow_state[:, -1:]], axis=1)
    spread = below_x + above_x + below_y + above_y + below_z + above_z - 6.0 * flow_state
    return flow_state + advect_number * (below_x - flow_state) + diffusion[None] * spread


def wall_columns(flow_state):
    points = flow_state.shape[2] * flow_state.shape[3]
    inputs = flow_state[0:4, 0:3].reshape(12, points)
    targets = jnp.stack(
        [flow_state[1, 4] - flow_state[1, 3], flow_state[3, 4] - flow_state[3, 3]]
    ).reshape(2, points)
    return jnp.concatenate([inputs, targets], axis=0).astype(jnp.bfloat16)


def apply_wall(advanced, new_stress):
    advanced = advanced.at[1, 0].add(-wall_gain * new_stress[0])
    return advanced.at[3, 0].add(-wall_gain * new_stress[1])


def contract_first(left, right):
    return lax.dot_general(
        left, right, (((0,), (0,)), ((), ())), preferred_element_type=jnp.float32
    )


def contract_last(left, right):
    return lax.dot_general(
        left, right, (((1,), (1,)), ((), ())), preferred_element_type=jnp.float32
    )


def body(
    flow_state,
    diffusion,
    wall_stress,
    batch_counts,
    batch_routes,
    wall_index,
    input_weight,
    middle_weight,
    output_weight,
):
    tile_count, capacity = wall_index.shape
    devices = lax.axis_size(("sec", "dev"))
    channels = 14
    slot_total = devices * SLOTS
    row_total = slot_total * capacity
    points = flow_state.shape[2] * flow_state.shape[3]
    columns = wall_columns(flow_state)
    picked = jnp.take(columns, wall_index.reshape(-1), axis=1).reshape(
        channels, tile_count, capacity
    )
    is_live = (
        jnp.arange(capacity, dtype=jnp.int32)[None, :] < batch_counts.reshape(tile_count)[:, None]
    )
    picked = jnp.where(is_live[None], picked, jnp.zeros((), jnp.bfloat16))
    destination = batch_routes.reshape(tile_count)
    matches = (destination[:, None] == jnp.arange(devices, dtype=jnp.int32)[None, :]).astype(
        jnp.int32
    )
    slot_rank = jnp.sum((jnp.cumsum(matches, axis=0) - matches) * matches, axis=1)
    slot_id = destination * SLOTS + slot_rank
    placing = (slot_id[:, None] == jnp.arange(slot_total, dtype=jnp.int32)[None, :]).astype(
        jnp.bfloat16
    )
    send_rows = jnp.einsum(
        "bs,cbk->sck", placing, picked, preferred_element_type=jnp.float32
    ).astype(jnp.bfloat16)
    send_rows = send_rows.reshape(devices, SLOTS, channels, capacity)
    send_live = jnp.einsum(
        "bs,bk->sk", placing, is_live.astype(jnp.bfloat16), preferred_element_type=jnp.float32
    ).astype(jnp.bfloat16)
    send_live = send_live.reshape(devices, SLOTS, capacity)
    got_rows, got_live = (
        lax.all_to_all(send_rows, ("sec", "dev"), split_axis=0, concat_axis=0, tiled=True),
        lax.all_to_all(send_live, ("sec", "dev"), split_axis=0, concat_axis=0, tiled=True),
    )
    sample_rows = jnp.transpose(got_rows, (0, 1, 3, 2)).reshape(row_total, channels)
    features = sample_rows[:, :12]
    targets = sample_rows[:, 12:].astype(jnp.float32)
    live_rows = got_live.reshape(row_total).astype(jnp.float32)
    pre_first = jnp.dot(features, input_weight, preferred_element_type=jnp.float32)
    first_tanh = jnp.tanh(pre_first)
    first_act = first_tanh.astype(jnp.bfloat16)
    part = first_act
    pre_second = jnp.dot(
        part,
        lax.all_gather(middle_weight, ("sec", "dev"), axis=0, tiled=True),
        preferred_element_type=jnp.float32,
    )
    second_tanh = jnp.tanh(pre_second)
    second_act = second_tanh.astype(jnp.bfloat16)
    prediction = contract_last(second_act, output_weight)
    errors = (prediction - targets) * live_rows[:, None]
    sent_back = jnp.transpose(
        prediction.astype(jnp.bfloat16).reshape(devices, SLOTS, capacity, 2), (0, 1, 3, 2)
    )
    answers = lax.all_to_all(sent_back, ("sec", "dev"), split_axis=0, concat_axis=0, tiled=True)
    answers = answers.reshape(slot_total, 2, capacity)
    live_total = jnp.sum(live_rows)
    batch_loss = (0.5 * jnp.sum(errors * errors) / live_total).reshape(1)
    live_dev = 5 * tile_count * capacity // 8
    scale = grad_number / math.sqrt(live_dev * devices)
    back_out = (errors * scale).astype(jnp.bfloat16)
    back_second = (
        jnp.dot(back_out, output_weight, preferred_element_type=jnp.float32)
        * (1.0 - second_tanh * second_tanh)
    ).astype(jnp.bfloat16)
    back_hidden = contract_last(
        back_second, lax.all_gather(middle_weight, ("sec", "dev"), axis=0, tiled=True)
    )
    back_first = (back_hidden * (1.0 - first_tanh * first_tanh)).astype(jnp.bfloat16)
    part = first_act
    grad_w_mid = lax.psum_scatter(
        contract_first(part, back_second), ("sec", "dev"), scatter_dimension=0, tiled=True
    )
    grad_w_in = lax.psum(contract_first(features, back_first), ("sec", "dev"))
    per_tile = jnp.einsum("bs,sck->cbk", placing, answers, preferred_element_type=jnp.float32)
    target_index = jnp.where(is_live, wall_index, points).reshape(-1)
    new_stress = (
        wall_stress.reshape(2, points)
        .at[:, target_index]
        .set(per_tile.reshape(2, -1), mode="drop")
        .reshape(wall_stress.shape)
    )
    padded = extended(flow_state.astype(jnp.bfloat16), ((("sec", "dev"), 2),), 1).astype(
        flow_state.dtype
    )
    advanced = advance(flow_state, diffusion, padded[:, :, :-2], padded[:, :, 2:])
    new_field = apply_wall(advanced, new_stress)
    return (new_field, new_stress, batch_loss, grad_w_in, grad_w_mid)


def solution(mesh):
    in_specs = (
        P(None, None, ("sec", "dev"), None),
        P(None, ("sec", "dev"), None),
        P(None, ("sec", "dev"), None),
        P(("sec", "dev"), None),
        P(("sec", "dev"), None),
        P(("sec", "dev"), None),
        P(),
        P(("sec", "dev"), None),
        P(),
    )
    out_specs = (
        P(None, None, ("sec", "dev"), None),
        P(None, ("sec", "dev"), None),
        P(("sec", "dev")),
        P(),
        P(("sec", "dev"), None),
    )
    return jax.shard_map(body, mesh=mesh, in_specs=in_specs, out_specs=out_specs, check_vma=False)
```

profile of v0, /device:TPU:24, one launch (start us, length us, event | category | flops | bytes accessed | tf_op | source)
XLA Modules:
  0.0 1081.5 jit_solution(13792528730048867405)
XLA Ops:
  7.2 0.7 all-gather.2.cloned.1.call-update
  7.9 0.8 iota_compare_fusion.2
  9.0 0.9 fusion.21
  9.9 0.7 multiply_add_fusion
  10.6 0.9 convolution_convert_fusion.1
  11.5 0.8 copy.53
  12.3 10.3 all-to-all-start.2
  22.5 3.0 convert_element_type.53
  25.9 1.0 slice.172
  27.0 0.3 copy.57
  27.3 0.2 pad_maximum_fusion.1
  27.5 3.3 copy.42
  30.9 4.3 gather_fusion
  35.4 0.2 convolution_convert_fusion
  35.8 0.9 copy.45
  36.7 9.8 all-to-all-start
  46.5 0.2 all-reduce.3.cloned.1.call-start
  46.9 9.9 all-to-all-done
  57.1 4.5 fusion.13
  61.6 153.5 %all-gather.2.cloned.1.call-done = bf16[2048,2048]{1,0:T(8,128)(2,1)} async-done(((bf16[16,2048]{1,0:T(8,128)(2,1)}), bf16[2048,2048]{1,0:T(8,128)(2,1)}) %all-gather.2.cloned.1.call-update) | async-done | bytes 8388624 | tf_op jit(solution)/shard_map/all_gather | solution.py:121
  215.1 13.7 %fusion.11 = f32[1024,2048]{1,0:T(8,128)S(1)} fusion(bf16[2048,2048]{1,0:T(8,128)(2,1)} %all-gather.2.cloned.1.call-done, f32[1024,2048]{1,0:T(8,128)} %fusion.13), kind=kOutput, calls=%fused_computation.24 | convolution fusion | flops 8592031744 | bytes 25165824 | tf_op jit(solution)/shard_map/dot_general | solution.py:119
  228.8 1.8 multiply_reduce_fusion
  230.6 3.6 multiply_convert_fusion.1
  234.3 14.9 %fusion.2 = f32[12,2048]{1,0:T(8,128)} fusion(f32[1024,2048]{1,0:T(8,128)} %fusion.13, bf16[1024,2048]{1,0:T(8,128)(2,1)} %multiply_convert_fusion.1, bf16[2048,2048]{1,0:T(8,128)(2,1)} %all-gather.2.cloned.1.call-done, bf16[1024,14]{1,0:T(8,128)(2,1)S(1)} %bitcast.59), kind=kOutput, calls=%fused_computation.10 | convolution fusion | flops 8648654848 | bytes 21098496 | tf_op jit(solution)/shard_map/dot_general | solution.py:54
  249.1 0.3 reduce-scatter.2.cloned.1.call-start
  249.4 15.9 %fusion.10 = f32[2048,2048]{1,0:T(8,128)} fusion(bf16[1024,2048]{1,0:T(8,128)(2,1)} %multiply_convert_fusion.1, f32[1024,2048]{1,0:T(8,128)} %fusion.13), kind=kOutput, calls=%fused_computation.23 | convolution fusion | flops 8592031744 | bytes 29360128 | tf_op jit(solution)/shard_map/dot_general | solution.py:54
  265.3 1.9 fusion.46
  267.2 7.5 collective-permute-start.1
  274.9 4.6 copy.37
  279.6 0.9 fusion.45
  280.5 1.1 fusion.42
  281.6 2.8 fusion.44
  284.4 3.4 fusion.43
  287.8 0.7 convert_reduce_fusion
  288.6 3.4 maximum_convert_fusion
  292.0 0.3 reshape.309
  292.3 0.7 copy.47
  293.0 4.4 all-to-all-start.1
  297.5 9.1 fusion.7
  308.1 0.2 convolution_bitcast_fusion
  308.8 10.7 scatter_fusion
  319.5 5.8 copy.54
  325.4 12.2 %fusion = (f32[16384]{0:T(1024)S(1)}, f32[16384]{0:T(1024)S(1)}) fusion(f32[2,16384]{0,1:T(8,128)} %scatter_fusion), kind=kLoop, calls=%fused_computation.3 | loop fusion | flops 32768 | bytes 262144 | tf_op jit(solution)/shard_map/mul | solution.py:50
  337.6 1.5 fusion.26
  339.1 1.5 fusion.25
  340.6 46.9 %all-reduce.3.cloned.1.call-done = f32[12,2048]{1,0:T(8,128)} async-done(((f32[12,2048]{1,0:T(8,128)}), f32[12,2048]{1,0:T(8,128)}) %all-reduce.3.cloned.1.call-update) | async-done | bytes 98320 | tf_op jit(solution)/shard_map/psum | solution.py:150
  387.5 684.8 %reduce-scatter.2.cloned.1.call-done = f32[16,2048]{1,0:T(8,128)} async-done(((f32[2048,2048]{1,0:T(8,128)}), f32[16,2048]{1,0:T(8,128)}) %reduce-scatter.2.cloned.1.call-update) | async-done | bytes 131088 | tf_op jit(solution)/shard_map/reduce_scatter | solution.py:147
  1072.3 1.6 copy.66
  (57 shorter events, 2.5 us)
Async XLA Ops:
  7.2 50.0 %copy-start = (bf16[12,2048]{1,0:T(8,128)(2,1)S(1)}, bf16[12,2048]{1,0:T(8,128)(2,1)}, u32[]{:S(2)}) copy-start(bf16[12,2048]{1,0:T(8,128)(2,1)} %param.19) | copy-start | bytes 147460
  7.2 18.3 %copy-start.2 = (f32[5,8,32,512]{3,2,1,0:T(8,128)S(1)}, f32[5,8,32,512]{3,2,1,0:T(8,128)}, u32[]{:S(2)}) copy-start(f32[5,8,32,512]{3,2,1,0:T(8,128)} %param.13) | copy-start | bytes 7864324
  7.2 18.5 %copy-start.5 = (s32[192,4]{0,1:T(4,128)S(1)}, s32[192,4]{0,1:T(4,128)}, u32[]{:S(2)}) copy-start(s32[192,4]{0,1:T(4,128)} %param.18) | copy-start | bytes 9220
  7.2 207.9 %all-gather.2.cloned.1.call-start = ((), (), s32[]{:S(2)}) async-start(), calls=%async_computation.4 | async-start | bytes 8454144 | tf_op jit(solution)/shard_map/all_gather | solution.py:121
  12.3 24.5 %all-to-all-start.2 = ((bf16[128,2,4]{2,1,0:T(2,128)(2,1)}), bf16[128,2,4]{2,1,0:T(2,128)(2,1)S(1)}, u32[]{:S(2)}, u32[]{:S(2)}) async-start(bf16[128,2,4]{2,1,0:T(2,128)(2,1)} %bitcast.20), calls=%async_computation.2 | async-start | bytes 131072 | tf_op jit(solution)/shard_map/all_to_all | solution.py:109
  27.3 8.1 copy-start.7
  36.7 20.0 %all-to-all-start = ((bf16[128,2,14,4]{2,1,3,0:T(2,128)(2,1)}), bf16[128,2,14,4]{2,1,3,0:T(2,128)(2,1)S(1)}, u32[]{:S(2)}, u32[]{:S(2)}) async-start(bf16[128,2,14,4]{2,1,3,0:T(2,128)(2,1)} %copy.45), calls=%async_computation | async-start | bytes 524288 | tf_op jit(solution)/shard_map/all_to_all | solution.py:108
  46.5 340.9 %all-reduce.3.cloned.1.call-start = ((), (), s32[]{:S(2)}) async-start(), calls=%async_computation.5 | async-start | bytes 262144 | tf_op jit(solution)/shard_map/psum | solution.py:150
  61.6 167.2 %copy-start.6 = (bf16[2,2048]{1,0:T(2,128)(2,1)S(1)}, bf16[2,2048]{1,0:T(2,128)(2,1)}, u32[]{:S(2)}) copy-start(bf16[2,2048]{1,0:T(2,128)(2,1)} %param.21) | copy-start | bytes 24580
  249.1 823.2 %reduce-scatter.2.cloned.1.call-start = ((), (), s32[]{:S(2)}) async-start(), calls=%async_computation.6 | async-start | bytes 16908288 | tf_op jit(solution)/shard_map/reduce_scatter | solution.py:147
  265.3 9.6 copy-start.4
  267.2 21.4 %collective-permute-start = (bf16[5,8,1,512]{3,2,1,0:T(2,128)(2,1)}, bf16[5,8,1,512]{3,2,1,0:T(2,128)(2,1)}, u32[]{:S(2)}, u32[]{:S(2)}) collective-permute-start(bf16[5,8,1,512]{3,2,1,0:T(2,128)(2,1)} %get-tuple-element.56), channel_id=1, source_target_pairs={{0,1},{1,2},{2,3},{3,4},{4,5},{5,6},{6,7},{7,8},{8,9},{9,10},{10,1... | collective-permute-start | bytes 122888 | tf_op jit(solution)/shard_map/ppermute | solution.py:22
  267.2 21.4 %collective-permute-start.1 = (bf16[5,8,1,512]{3,2,1,0:T(2,128)(2,1)S(1)}, bf16[5,8,1,512]{3,2,1,0:T(2,128)(2,1)}, u32[]{:S(2)}, u32[]{:S(2)}) collective-permute-start(bf16[5,8,1,512]{3,2,1,0:T(2,128)(2,1)S(1)} %get-tuple-element.57), channel_id=1, source_target_pairs={{1,0},{2,1},{3,2},{4,3},{5,4},{6,5},{7,6},{8,7},{9,8},{10,9},{11,1... | collective-permute-start | bytes 122888 | tf_op jit(solution)/shard_map/ppermute | solution.py:25
  284.4 4.2 copy-start.3
  293.0 14.9 %all-to-all-start.1 = ((bf16[128,2,2,4]{3,1,2,0:T(2,128)(2,1)}), bf16[128,2,2,4]{3,1,2,0:T(2,128)(2,1)S(1)}, u32[]{:S(2)}, u32[]{:S(2)}) async-start(bf16[128,2,2,4]{3,1,2,0:T(2,128)(2,1)} %copy.47), calls=%async_computation.1 | async-start | bytes 262144 | tf_op jit(solution)/shard_map/all_to_all | solution.py:131
  325.4 748.5 %copy-start.1 = (bf16[12,2048]{1,0:T(8,128)(2,1)S(1)}, bf16[12,2048]{1,0:T(8,128)(2,1)}, u32[]{:S(2)}) copy-start(bf16[12,2048]{1,0:T(8,128)(2,1)} %param.19) | copy-start | bytes 147460
Sparse Core Ops, SparseCore 0:
  9.8 205.3 all-gather.1
  249.3 138.1 all-reduce.2
  390.6 681.7 reduce-scatter.1
where the time goes:
time: 1080 us
  waiting for transfers between devices  896 us (83%)
  matrix products  55.6 us (5%)
  local copies, waits for them, and re-layouts  46.7 us (4%)
  other arithmetic  34.3 us (3%)
  starting transfers between devices  32.5 us (3%)
  between operations  16.5 us (2%)
    reduce_scatter x1, waiting for transfers between devices, body(): lax.psum_scatter(contract_first(part, back_second), ('sec', 'dev'), scatt...  685 us
    all_gather x1, waiting for transfers between devices, body(): lax.all_gather(middle_weight, ('sec', 'dev'), axis=0, tiled=True)  154 us
    psum x1, waiting for transfers between devices, body(): grad_w_in = lax.psum(contract_first(features, back_first), ('sec', 'dev'))  46.9 us
    dot_general x2, matrix products, contract_first(): lax.dot_general(left, right, (((0,), (0,)), ((), ())), preferred_element_...  30.7 us
  transfers between devices with their start and end apart: 8, of which 4 were waited for; matrix products, arithmetic and copies ran while one was open for 9% of the time, Pallas kernels for 0%

commit v1 on v0

v1 whole, which is shorter than its diff:
```python
import math

import jax
import jax.numpy as jnp
from jax import lax
from jax.experimental import pallas as pl
from jax.experimental.pallas import tpu as pltpu
from jax.sharding import PartitionSpec as P

BF = jnp.bfloat16
F32 = jnp.float32
MESH = pl.DeviceIdType.MESH

H = 2048
CAP = 4
TILES = 192
LIVE = 480
PAD = 512
GROUP = 8
COLS = H // GROUP
S = GROUP * LIVE
CH = 1280
NCH = S // CH
JT = 512
DEVICES = 128
ADVECT = 0.3
GAIN = 0.5
SCALE = 32.0 / math.sqrt(LIVE * DEVICES)


def nn(a, b):
    return jnp.dot(a, b, preferred_element_type=F32)


def nt(a, b):
    return lax.dot_general(a, b, (((1,), (1,)), ((), ())), preferred_element_type=F32)


def tn(a, b):
    return lax.dot_general(a, b, (((0,), (0,)), ((), ())), preferred_element_type=F32)


def iota(shape, dim):
    return lax.broadcasted_iota(jnp.int32, shape, dim)


def train_kernel(
    flow, counts, routes, index, win, wmid, wout,
    halo_out, meta_out, small_out, gmid_out,
    t, fs, w, wct, d2, bst, gm, ra, rb, acc_a, acc_b, r2a, r2b, fin,
    planes, tplanes, edge, wsrc, wint, wpad, own, fbuf, ftot, feats, pbuf, rowmeta, perr,
    gwp, rg, rgx, rgy,
    lsem, ssem, rsem,
):
    sec = lax.axis_index("sec")
    dev = lax.axis_index("dev")
    m = dev % 8
    x = (dev // 8) % 4
    yh = dev // 32
    y = yh * 2 + sec
    yq = sec * 2 + yh
    flat = sec * 64 + dev
    used = [0]

    def send(src, dst, to):
        i = used[0]
        used[0] += 1
        copy = pltpu.make_async_remote_copy(
            src_ref=src, dst_ref=dst, send_sem=ssem.at[i], recv_sem=rsem.at[i],
            device_id=to, device_id_type=MESH,
        )
        copy.start()
        return copy

    members = [((m + k) % 8, (sec, dev - m + (m + k) % 8)) for k in range(1, 8)]
    xs = [((x + k) % 4, (sec, yh * 32 + ((x + k) % 4) * 8 + m)) for k in (1, 3, 2)]
    ys = []
    for k in (1, 3, 2):
        yy = (y + k) % 4
        ys.append(((yy % 2) * 2 + yy // 2, (yy % 2, (yy // 2) * 32 + x * 8 + m)))
    up = (flat + 1) % 128
    down = (flat + 127) % 128
    up_id = (up // 64, up % 64)
    down_id = (down // 64, down % 64)

    loads = [
        pltpu.make_async_copy(flow.at[0:4, 0:3], planes, lsem.at[0]),
        pltpu.make_async_copy(flow.at[1, 3:5], tplanes.at[0], lsem.at[1]),
        pltpu.make_async_copy(flow.at[3, 3:5], tplanes.at[1], lsem.at[2]),
        pltpu.make_async_copy(flow.at[:, :, 0:8, :], edge.at[0], lsem.at[3]),
        pltpu.make_async_copy(flow.at[:, :, 24:32, :], edge.at[1], lsem.at[4]),
    ]
    for copy in loads:
        copy.start()

    barrier = pltpu.get_barrier_semaphore()
    partners = [p for _, p in members] + [p for _, p in xs] + [p for _, p in ys] + [up_id, down_id]
    for p in partners:
        pl.semaphore_signal(barrier, inc=1, device_id=p, device_id_type=MESH)

    for i in range(GROUP):
        for h in range(2):
            wsrc[i, h] = wmid[:, COLS * i + 128 * h:COLS * i + 128 * h + 128]
    winp = jnp.concatenate([win[...].astype(F32), jnp.zeros((4, H), F32)], axis=0)
    wint[...] = winp.T.astype(BF)
    wpad[...] = jnp.zeros_like(wpad)
    wpad[0:2, :] = wout[:, pl.ds(pl.multiple_of(m * COLS, COLS), COLS)].astype(F32)

    pl.semaphore_wait(barrier, len(partners))

    mine = pl.ds(pl.multiple_of(m * 16, 16), 16)
    w0 = [send(wsrc.at[mm], w.at[:, yq, x, mine, :], to) for mm, to in members]
    w[:, yq, x, mine, :] = wsrc[m]

    for copy in loads:
        copy.wait()
    halo_src = own
    halo_src[0] = edge[0, :, :, 0, :]
    halo_src[1] = edge[1, :, :, 7, :]
    halos = [
        send(halo_src.at[0], halo_out.at[1], down_id),
        send(halo_src.at[1], halo_out.at[0], up_id),
    ]

    cnt = jnp.broadcast_to(counts[...].astype(F32), (16, TILES)).astype(BF)
    r_i, c_i = iota((TILES, TILES), 0), iota((TILES, TILES), 1)
    start = nt((c_i < r_i).astype(F32).astype(BF), cnt)[:, 0:1]
    ends = nt((c_i <= r_i).astype(F32).astype(BF), cnt)[:, 0:1]
    place = iota((TILES, PAD), 1).astype(F32)
    onehot = jnp.where((place >= start) & (place < ends), 1.0, 0.0).astype(BF)
    idx = index[...]
    lane16 = iota((TILES, 16), 1)
    table = jnp.zeros((TILES, 16), jnp.int32)
    start_i = start.astype(jnp.int32)
    pieces = []
    for k in range(CAP):
        col = idx[:, k:k + 1]
        pieces += [(k, col >> 9), (4 + k, (col >> 4) & 31), (8 + k, col & 15)]
    pieces += [(12, start_i >> 4), (13, start_i & 15), (14, routes[...])]
    for at, col in pieces:
        table = jnp.where(lane16 == at, col, table)
    vals = tn(table.astype(F32).astype(BF), onehot)
    lane = iota((1, PAD), 1)
    kk = lane.astype(F32) - (vals[12:13] * 16.0 + vals[13:14])
    zrow = jnp.zeros((1, PAD), F32)
    xrow = jnp.zeros((1, PAD), F32)
    for k in range(CAP):
        hit = kk == float(k)
        zrow = jnp.where(hit, vals[k:k + 1], zrow)
        xrow = jnp.where(hit, vals[4 + k:5 + k] * 16.0 + vals[8 + k:9 + k], xrow)
    valid = lane < LIVE
    zrow = jnp.where(valid, zrow, -1.0)
    xrow = jnp.where(valid, xrow, -1.0)
    rowmeta[0:1, :] = zrow
    rowmeta[1:2, :] = xrow
    rowmeta[2:3, :] = jnp.where(valid, vals[14:15], -1.0)
    oz = jnp.where(iota((32, PAD), 0).astype(F32) == zrow, 1.0, 0.0)
    ox = jnp.where(iota((PAD, PAD), 0).astype(F32) == xrow, 1.0, 0.0).astype(BF)
    tp = jnp.stack([tplanes[0, 1] - tplanes[0, 0], tplanes[1, 1] - tplanes[1, 0]])
    table_p = jnp.concatenate(
        [planes[...].reshape(384, PAD).astype(BF), tp.reshape(64, PAD).astype(BF)], axis=0
    )
    got = nn(table_p, ox).reshape(14, 32, PAD) * oz[None]
    picked = jnp.sum(got, axis=1)
    picked = jnp.concatenate([picked, jnp.zeros((2, PAD), F32)], axis=0)
    fbuf[m] = picked.astype(BF)
    fcopies = [send(fbuf.at[m], fbuf.at[m], to) for _, to in members]

    for copy in w0:
        copy.wait()
    w1 = [send(w.at[0, yq, x], w.at[0, yq, x], to) for _, to in xs]
    w1 += [send(w.at[1, yq, x], w.at[1, yq, x], to) for _, to in ys]

    for copy in fcopies:
        copy.wait()
    ftot[...] = jnp.zeros_like(ftot)
    for i in range(GROUP):
        base, rest = divmod(LIVE * i, 128)
        wide = jnp.concatenate([fbuf[i].astype(F32), jnp.zeros((16, 128), F32)], axis=1)
        if rest:
            wide = pltpu.roll(wide, rest, 1)
        ftot[:, 128 * base:128 * base + PAD + 128] += wide
    feats[...] = ftot[:, 0:S].astype(BF)

    for copy in w1:
        copy.wait()
    w2 = [send(w.at[0, yq], w.at[0, yq], to) for _, to in ys]
    w2 += [send(w.at[1, :, x], w.at[1, :, x], to) for _, to in xs]

    def first(q):
        sl = slice(CH * q, CH * q + CH)

        def inner(j, _):
            rows = pl.ds(pl.multiple_of(j * JT, JT), JT)
            act = jnp.tanh(nn(wint[rows, :], feats[:, sl]))
            t[rows, sl] = act
            fs[rows, :] = act.astype(BF)
            return 0

        lax.fori_loop(0, H // JT, inner, 0, unroll=True)

    for q in range(NCH):
        sl = slice(CH * q, CH * q + CH)
        first(q)
        if q == 0:
            for copy in w2:
                copy.wait()
            for h in range(2):
                wct[128 * h:128 * h + 128, :] = w[h].reshape(H, 128).astype(F32).T.astype(BF)
        act2 = jnp.tanh(nn(wct[...], fs[...]))
        d2[:, sl] = 1.0 - act2 * act2
        pbuf[m, 2 * q:2 * q + 2, :] = nn(wpad[...].astype(BF), act2.astype(BF))[0:2]
    pbuf[m, 6:8, :] = jnp.zeros((2, CH), F32)
    pcopies = [send(pbuf.at[m], pbuf.at[m], to) for _, to in members]
    for copy in pcopies:
        copy.wait()

    total = pbuf[0]
    for i in range(1, GROUP):
        total = total + pbuf[i]
    pred = jnp.concatenate([total[2 * q:2 * q + 2] for q in range(NCH)], axis=1)
    err = pred - ftot[12:14, 0:S]
    perr[0:2, :] = pred
    perr[2:4, :] = err
    perr[4:8, :] = jnp.zeros((4, S), F32)
    bo = (perr[...] * SCALE)
    bo = jnp.concatenate([bo[2:4], jnp.zeros((14, S), F32)], axis=0).astype(BF)
    for q in range(NCH):
        sl = slice(CH * q, CH * q + CH)
        bst[:, sl] = (tn(wpad[...].astype(BF), bo[:, sl]) * d2[:, sl]).astype(BF)

    def mid(q, _):
        rows = pl.ds(pl.multiple_of(q * JT, JT), JT)
        part = nt(t[rows, :].astype(BF), bst[...])
        for h in range(2):
            gm[h, q] = part[:, 128 * h:128 * h + 128].reshape(4, 128, 128)
        return 0

    lax.fori_loop(0, H // JT, mid, 0)
    s1 = [send(gm.at[0, :, xx], ra.at[i], to) for i, (xx, to) in enumerate(xs)]
    s1 += [send(gm.at[1, yy], rb.at[i], to) for i, (yy, to) in enumerate(ys)]

    rolled = pltpu.roll(perr[...], (S - LIVE * m) % S, 1)[:, 0:PAD]
    meta_out[0:2, :] = jnp.where(valid, rolled[0:2], 0.0)
    meta_out[2:4, :] = rowmeta[0:2, :]
    meta_out[4:8, :] = jnp.zeros((4, PAD), F32)
    square = rolled[2:3] * rolled[2:3] + rolled[3:4] * rolled[3:4]
    square = jnp.where(valid, square, 0.0)
    chosen = iota((DEVICES, PAD), 0).astype(F32) == rowmeta[2:3, :]
    loss_col = jnp.sum(jnp.where(chosen, square, 0.0), axis=1, keepdims=True)
    count_col = jnp.sum(jnp.where(chosen, 1.0, 0.0), axis=1, keepdims=True)
    loss_row = jnp.broadcast_to(loss_col, (DEVICES, DEVICES)).T[0:1]
    count_row = jnp.broadcast_to(count_col, (DEVICES, DEVICES)).T[0:1]

    def back(q, _):
        rows = pl.ds(pl.multiple_of(q * JT, JT), JT)
        wc = jnp.concatenate([w[0, q].reshape(JT, 128), w[1, q].reshape(JT, 128)], axis=1)
        acc = jnp.zeros((16, JT), F32)
        for s in range(NCH):
            sl = slice(CH * s, CH * s + CH)
            act = t[rows, sl]
            bf = (nn(wc, bst[:, sl]) * (1.0 - act * act)).astype(BF)
            acc = acc + nt(feats[:, sl], bf)
        gwp[:, rows] = acc
        return 0

    lax.fori_loop(0, H // JT, back, 0)
    gwp[12:16, :] = jnp.zeros((4, H), F32)
    gwp[12:13, 0:DEVICES] = loss_row
    gwp[13:14, 0:DEVICES] = count_row

    g1 = [
        send(gwp.at[:, pl.ds(pl.multiple_of(mm * COLS, COLS), COLS)], rg.at[i], to)
        for i, (mm, to) in enumerate(members)
    ]
    for copy in s1:
        copy.wait()
    acc_a[...] = gm[0, :, x] + ra[0] + ra[1] + ra[2]
    acc_b[...] = gm[1, yq] + rb[0] + rb[1] + rb[2]
    s2 = [send(acc_a.at[yy], r2a.at[i], to) for i, (yy, to) in enumerate(ys)]
    s2 += [send(acc_b.at[xx], r2b.at[i], to) for i, (xx, to) in enumerate(xs)]

    my_cols = pl.ds(pl.multiple_of(m * COLS, COLS), COLS)
    for copy in g1:
        copy.wait()
    part = gwp[:, my_cols]
    for i in range(7):
        part = part + rg[i]
    rgx[x] = part
    g2 = [send(rgx.at[x], rgx.at[x], to) for _, to in xs]
    for copy in g2:
        copy.wait()
    rgy[yq] = (rgx[0] + rgx[1]) + (rgx[2] + rgx[3])
    g3 = [send(rgy.at[yq], rgy.at[yq], to) for _, to in ys]

    for copy in s2:
        copy.wait()
    fin[0] = acc_a[yq] + r2a[0] + r2a[1] + r2a[2]
    fin[1] = acc_b[x] + r2b[0] + r2b[1] + r2b[2]
    s3 = [
        send(fin.at[:, pl.ds(pl.multiple_of(mm * 16, 16), 16), :], gmid_out.at[m], to)
        for mm, to in members
    ]
    gmid_out[m] = fin[:, mine, :]

    for copy in g3:
        copy.wait()
    small_out[m] = (rgy[0] + rgy[1]) + (rgy[2] + rgy[3])
    g4 = [send(small_out.at[m], small_out.at[m], to) for _, to in members]
    for copy in s3 + g4 + halos:
        copy.wait()


N_SENDS = 7 + 2 + 7 + 6 + 6 + 7 + 6 + 7 + 6 + 3 + 3 + 7 + 7


def train(flow, counts, routes, index, win, wmid, wout):
    vm = pl.BlockSpec(memory_space=pltpu.VMEM)
    sds = jax.ShapeDtypeStruct
    return pl.pallas_call(
        train_kernel,
        out_shape=(
            sds((2, 5, 8, 512), F32),
            sds((8, PAD), F32),
            sds((GROUP, 16, COLS), F32),
            sds((GROUP, 2, 16, 128), F32),
        ),
        in_specs=[pl.BlockSpec(memory_space=pl.ANY)] + [vm] * 6,
        out_specs=(vm,) * 4,
        scratch_shapes=[
            pltpu.VMEM((H, S), F32),
            pltpu.VMEM((H, CH), BF),
            pltpu.VMEM((2, 4, 4, 128, 128), BF),
            pltpu.VMEM((COLS, H), BF),
            pltpu.VMEM((COLS, S), F32),
            pltpu.VMEM((COLS, S), BF),
            pltpu.VMEM((2, 4, 4, 128, 128), F32),
            pltpu.VMEM((3, 4, 128, 128), F32),
            pltpu.VMEM((3, 4, 128, 128), F32),
            pltpu.VMEM((4, 128, 128), F32),
            pltpu.VMEM((4, 128, 128), F32),
            pltpu.VMEM((3, 128, 128), F32),
            pltpu.VMEM((3, 128, 128), F32),
            pltpu.VMEM((2, 128, 128), F32),
            pltpu.VMEM((4, 3, 32, 512), F32),
            pltpu.VMEM((2, 2, 32, 512), F32),
            pltpu.VMEM((2, 5, 8, 8, 512), F32),
            pltpu.VMEM((GROUP, 2, 16, 128), BF),
            pltpu.VMEM((H, 16), BF),
            pltpu.VMEM((16, COLS), F32),
            pltpu.VMEM((2, 5, 8, 512), F32),
            pltpu.VMEM((GROUP, 16, PAD), BF),
            pltpu.VMEM((16, S + 128), F32),
            pltpu.VMEM((16, S), BF),
            pltpu.VMEM((GROUP, 8, CH), F32),
            pltpu.VMEM((8, PAD), F32),
            pltpu.VMEM((8, S), F32),
            pltpu.VMEM((16, H), F32),
            pltpu.VMEM((7, 16, COLS), F32),
            pltpu.VMEM((4, 16, COLS), F32),
            pltpu.VMEM((4, 16, COLS), F32),
            pltpu.SemaphoreType.DMA((5,)),
            pltpu.SemaphoreType.DMA((N_SENDS,)),
            pltpu.SemaphoreType.DMA((N_SENDS,)),
        ],
        compiler_params=pltpu.CompilerParams(
            collective_id=0, has_side_effects=True, vmem_limit_bytes=62 * 2**20
        ),
        name="train",
    )(flow, counts, routes, index, win, wmid, wout)


def slab_kernel(flow, diff, stress, halo, meta, small, gmid, field, new_stress, loss, gw, gwm):
    v = pl.program_id(0)

    @pl.when(v == 0)
    def _():
        zrow, xrow = meta[2:3, :], meta[3:4, :]
        oz = jnp.where(iota((32, PAD), 0).astype(F32) == zrow, 1.0, 0.0)
        ox = jnp.where(iota((PAD, PAD), 0).astype(F32) == xrow, 1.0, 0.0).astype(BF)
        lhs = jnp.concatenate([oz * meta[0:1, :], oz * meta[1:2, :], oz], axis=0).astype(BF)
        spread = nt(lhs, ox)
        hit = spread[64:96] > 0.5
        new_stress[0] = jnp.where(hit, spread[0:32], stress[0])
        new_stress[1] = jnp.where(hit, spread[32:64], stress[1])
        me = lax.axis_index("sec") * 64 + lax.axis_index("dev")
        ratio = 0.5 * small[0, 12:13, 0:DEVICES] / small[0, 13:14, 0:DEVICES]
        loss[0] = jnp.sum(jnp.where(iota((1, DEVICES), 1) == me, ratio, 0.0))
        for i in range(GROUP):
            gw[:, COLS * i:COLS * i + COLS] = small[i, 0:12, :]
            for h in range(2):
                at = COLS * i + 128 * h
                gwm[:, at:at + 128] = gmid[i, h]

    u = flow[0]
    row, col = iota((8, 32, 512), 1), iota((8, 32, 512), 2)
    below_z = jnp.where(row == 0, halo[0, v][:, None, :], pltpu.roll(u, 1, 1))
    above_z = jnp.where(row == 31, halo[1, v][:, None, :], pltpu.roll(u, 31, 1))
    below_x = jnp.where(col == 0, u, pltpu.roll(u, 1, 2))
    above_x = jnp.where(col == 511, u, pltpu.roll(u, 511, 2))
    below_y = jnp.concatenate([u[0:1], u[0:7]], axis=0)
    above_y = jnp.concatenate([u[1:8], u[7:8]], axis=0)
    spread = below_x + above_x + below_y + above_y + below_z + above_z - 6.0 * u
    field[0] = u + ADVECT * (below_x - u) + diff[...] * spread

    @pl.when(v == 1)
    def _():
        field[0, 0] = field[0, 0] - GAIN * new_stress[0]

    @pl.when(v == 3)
    def _():
        field[0, 0] = field[0, 0] - GAIN * new_stress[1]


def slab(flow, diff, stress, halo, meta, small, gmid):
    sds = jax.ShapeDtypeStruct

    def whole(shape):
        return pl.BlockSpec(shape, lambda v: (0,) * len(shape))

    block = pl.BlockSpec((1, 8, 32, 512), lambda v: (v, 0, 0, 0))
    return pl.pallas_call(
        slab_kernel,
        grid=(5,),
        out_shape=(
            sds((5, 8, 32, 512), F32),
            sds((2, 32, 512), F32),
            sds((1,), F32),
            sds((12, H), F32),
            sds((16, H), F32),
        ),
        in_specs=[
            block, whole((8, 32, 512)), whole((2, 32, 512)), whole((2, 5, 8, 512)),
            whole((8, PAD)), whole((GROUP, 16, COLS)), whole((GROUP, 2, 16, 128)),
        ],
        out_specs=(
            block, whole((2, 32, 512)), pl.BlockSpec(memory_space=pltpu.SMEM),
            whole((12, H)), whole((16, H)),
        ),
        compiler_params=pltpu.CompilerParams(vmem_limit_bytes=32 * 2**20),
        name="slab",
    )(flow, diff, stress, halo, meta, small, gmid)


def body(flow, diff, stress, counts, routes, index, win, wmid, wout):
    halo, meta, small, gmid = train(flow, counts, routes, index, win, wmid, wout)
    return slab(flow, diff, stress, halo, meta, small, gmid)


def solution(mesh):
    both = ("sec", "dev")
    in_specs = (
        P(None, None, both, None), P(None, both, None), P(None, both, None),
        P(both, None), P(both, None), P(both, None), P(), P(both, None), P(),
    )
    out_specs = (P(None, None, both, None), P(None, both, None), P(both), P(), P(both, None))
    return jax.shard_map(body, mesh=mesh, in_specs=in_specs, out_specs=out_specs, check_vma=False)
```

time: 1080 us -> 89.3 us (0.08)
  the two profiles are of different devices: /device:TPU:24 before, /device:TPU:1 now
where the time goes in v1:
time: 89.3 us; the launch traced here: 88.9 us
  Pallas kernels  80 us (90%)
  local copies, waits for them, and re-layouts  8.14 us (9%)
    pallas_call x1, Pallas kernels, train(): pl.pallas_call(train_kernel, out_shape=(sds((2, 5, 8, 512), F32), sds((8,...  75.6 us
    unnamed x16, local copies, waits for them, and re-layouts  8.14 us
    pallas_call x1, Pallas kernels, slab(): pl.pallas_call(slab_kernel, grid=(5,), out_shape=(sds((5, 8, 32, 512), F3...  4.36 us

profile of v1, /device:TPU:1, one launch (start us, length us, event | category | flops | bytes accessed | tf_op | source)
XLA Modules:
  0.0 88.9 jit_solution(3593342366854830775)
XLA Ops:
  0.6 0.0 copy-start.3
  0.6 0.0 copy-start.1
  0.7 1.5 %copy.14.routes = s32[192,1]{1,0:T(8,128)} copy(s32[192,1]{0,1:T(1,128)} %param.13) | data formatting | bytes 1536 | tf_op args[4]
  2.2 1.4 %copy.15.index = s32[192,4]{1,0:T(8,128)} copy(s32[192,4]{0,1:T(4,128)} %param.14) | data formatting | bytes 6144 | tf_op args[5]
  3.6 75.6 %train.1 = (f32[2,5,8,512]{3,2,1,0:T(8,128)}, f32[8,512]{1,0:T(8,128)}, f32[8,16,256]{2,1,0:T(8,128)}, f32[8,2,16,128]{3,2,1,0:T(8,128)}) custom-call(f32[5,8,32,512]{3,2,1,0:T(8,128)} %flow.3, s32[1,192]{1,0:T(1,128)} %counts.1, s32[192,1]{1,0:T(8,128)} %copy.14.routes, s32[192,4]{1,0:T(8,128)} %copy.15.index, bf16[12,2048]{1,0:T(8,128)(2,1)} %win.1, ...), custom_call_target="tpu_custom_call" | custom-call | tf_op jit(solution)/shard_map/train/pallas_call | solution.py:320
  79.2 0.0 copy-done.3
  79.2 0.0 copy-done.1
  79.2 0.0 copy-start
  79.3 1.7 %copy-done = f32[5,8,32,512]{3,2,1,0:T(8,128)S(1)} copy-done((f32[5,8,32,512]{3,2,1,0:T(8,128)S(1)}, f32[5,8,32,512]{3,2,1,0:T(8,128)}, u32[]{:S(2)}) %copy-start) | copy-done | bytes 2621464
  81.0 0.0 copy-start.2
  81.0 0.9 %copy-done.2 = f32[2,5,8,512]{3,2,1,0:T(8,128)S(1)} copy-done((f32[2,5,8,512]{3,2,1,0:T(8,128)S(1)}, f32[2,5,8,512]{3,2,1,0:T(8,128)}, u32[]{:S(2)}) %copy-start.2) | copy-done | bytes 163864
  81.9 0.0 copy-start.4
  81.9 0.9 %copy-done.4 = f32[8,16,256]{2,1,0:T(8,128)S(1)} copy-done((f32[8,16,256]{2,1,0:T(8,128)S(1)}, f32[8,16,256]{2,1,0:T(8,128)}, u32[]{:S(2)}) %copy-start.4) | copy-done | bytes 131096
  82.8 0.0 copy-start.5
  82.8 0.9 %copy-done.5 = f32[8,2,16,128]{3,2,1,0:T(8,128)S(1)} copy-done((f32[8,2,16,128]{3,2,1,0:T(8,128)S(1)}, f32[8,2,16,128]{3,2,1,0:T(8,128)}, u32[]{:S(2)}) %copy-start.5) | copy-done | bytes 131096
  83.7 0.0 copy-start.6
  83.7 0.7 copy-done.6
  84.4 4.4 %slab.1 = (f32[5,8,32,512]{3,2,1,0:T(8,128)}, f32[2,32,512]{2,1,0:T(8,128)}, f32[1]{0:T(128)}, f32[12,2048]{1,0:T(8,128)}, f32[16,2048]{1,0:T(8,128)}) custom-call(f32[5,8,32,512]{3,2,1,0:T(8,128)S(1)} %copy-done, f32[8,32,512]{2,1,0:T(8,128)S(1)} %copy-done.1, f32[2,32,512]{2,1,0:T(8,128)S(1)} %copy-done.3, f32[2,5,8,512]{3,2,1,0:T(8,128)S(1)} %copy-done.2, ...), custom_call_target="tpu_custom_call" | custom-call | tf_op jit(solution)/shard_map/slab/pallas_call | solution.py:422
Async XLA Ops:
  0.6 78.6 %copy-start.3 = (f32[2,32,512]{2,1,0:T(8,128)S(1)}, f32[2,32,512]{2,1,0:T(8,128)}, u32[]{:S(2)}) copy-start(f32[2,32,512]{2,1,0:T(8,128)} %stress.1) | copy-start | bytes 393220
  0.6 78.6 %copy-start.1 = (f32[8,32,512]{2,1,0:T(8,128)S(1)}, f32[8,32,512]{2,1,0:T(8,128)}, u32[]{:S(2)}) copy-start(f32[8,32,512]{2,1,0:T(8,128)} %diff.1) | copy-start | bytes 1572868
  79.2 1.7 %copy-start = (f32[5,8,32,512]{3,2,1,0:T(8,128)S(1)}, f32[5,8,32,512]{3,2,1,0:T(8,128)}, u32[]{:S(2)}) copy-start(f32[5,8,32,512]{3,2,1,0:T(8,128)} %flow.3) | copy-start | bytes 7864324
  81.0 0.9 %copy-start.2 = (f32[2,5,8,512]{3,2,1,0:T(8,128)S(1)}, f32[2,5,8,512]{3,2,1,0:T(8,128)}, u32[]{:S(2)}) copy-start(f32[2,5,8,512]{3,2,1,0:T(8,128)} %get-tuple-element.9.halo) | copy-start | bytes 491524
  81.9 0.9 %copy-start.4 = (f32[8,16,256]{2,1,0:T(8,128)S(1)}, f32[8,16,256]{2,1,0:T(8,128)}, u32[]{:S(2)}) copy-start(f32[8,16,256]{2,1,0:T(8,128)} %get-tuple-element.11.small) | copy-start | bytes 393220
  82.8 0.9 %copy-start.5 = (f32[8,2,16,128]{3,2,1,0:T(8,128)S(1)}, f32[8,2,16,128]{3,2,1,0:T(8,128)}, u32[]{:S(2)}) copy-start(f32[8,2,16,128]{3,2,1,0:T(8,128)} %get-tuple-element.12.gmid) | copy-start | bytes 393220
  83.7 0.7 copy-start.6

commit v2 on v1

--- a/solution.py
+++ b/solution.py
@@ -21,6 +21,7 @@
 S = GROUP * LIVE
 CH = 1280
 NCH = S // CH
+PARTS = ((0, 1280, 0), (1280, 640, 1280), (1920, 1280, 0), (3200, 640, 1280))
 JT = 512
 DEVICES = 128
 ADVECT = 0.3
@@ -45,11 +46,11 @@
 
 
 def train_kernel(
-    flow, counts, routes, index, win, wmid, wout,
+    flow, counts_h, routes_h, index_h, win_h, wmid_h, wout_h,
     halo_out, meta_out, small_out, gmid_out,
-    t, fs, w, wct, d2, bst, gm, ra, rb, acc_a, acc_b, r2a, r2b, fin,
-    planes, tplanes, edge, wsrc, wint, wpad, own, fbuf, ftot, feats, pbuf, rowmeta, perr,
-    gwp, rg, rgx, rgy,
+    t, fs, w, wct, d2, bst, gm, ra, rb, r2a, r2b, fin,
+    planes, tplanes, wsrc, wint, wpad, own, fbuf, ftot, feats, pbuf, rowmeta, perr,
+    gwp, rg, rgp, counts, routes, index, win, wmid, wout, table,
     lsem, ssem, rsem,
 ):
     sec = lax.axis_index("sec")
@@ -72,31 +73,40 @@
         copy.start()
         return copy
 
+    def at_plane(yy, xx):
+        return (yy % 2, (yy // 2) * 32 + xx * 8 + m)
+
     members = [((m + k) % 8, (sec, dev - m + (m + k) % 8)) for k in range(1, 8)]
-    xs = [((x + k) % 4, (sec, yh * 32 + ((x + k) % 4) * 8 + m)) for k in (1, 3, 2)]
+    xs = [((x + k) % 4, at_plane(y, (x + k) % 4)) for k in (1, 3, 2)]
     ys = []
     for k in (1, 3, 2):
         yy = (y + k) % 4
-        ys.append(((yy % 2) * 2 + yy // 2, (yy % 2, (yy // 2) * 32 + x * 8 + m)))
+        ys.append(((yy % 2) * 2 + yy // 2, at_plane(yy, x)))
+    plane = [
+        at_plane((y + a) % 4, (x + b) % 4) for a in range(4) for b in range(4) if a or b
+    ]
     up = (flat + 1) % 128
     down = (flat + 127) % 128
     up_id = (up // 64, up % 64)
     down_id = (down // 64, down % 64)
 
-    loads = [
-        pltpu.make_async_copy(flow.at[0:4, 0:3], planes, lsem.at[0]),
-        pltpu.make_async_copy(flow.at[1, 3:5], tplanes.at[0], lsem.at[1]),
-        pltpu.make_async_copy(flow.at[3, 3:5], tplanes.at[1], lsem.at[2]),
-        pltpu.make_async_copy(flow.at[:, :, 0:8, :], edge.at[0], lsem.at[3]),
-        pltpu.make_async_copy(flow.at[:, :, 24:32, :], edge.at[1], lsem.at[4]),
+    barrier = pltpu.get_barrier_semaphore()
+    partners = [p for _, p in members] + plane + [up_id, down_id]
+    for p in partners:
+        pl.semaphore_signal(barrier, inc=1, device_id=p, device_id_type=MESH)
+
+    pairs = [
+        (counts_h, counts), (routes_h, routes), (index_h, index), (win_h, win),
+        (wout_h, wout), (wmid_h, wmid),
+        (flow.at[0:4, 0:3], planes), (flow.at[1, 3:5], tplanes.at[0]),
+        (flow.at[3, 3:5], tplanes.at[1]), (flow.at[:, :, 0, :], own.at[0]),
+        (flow.at[:, :, 31, :], own.at[1]),
     ]
+    loads = [pltpu.make_async_copy(a, b, lsem.at[i]) for i, (a, b) in enumerate(pairs)]
     for copy in loads:
         copy.start()
-
-    barrier = pltpu.get_barrier_semaphore()
-    partners = [p for _, p in members] + [p for _, p in xs] + [p for _, p in ys] + [up_id, down_id]
-    for p in partners:
-        pl.semaphore_signal(barrier, inc=1, device_id=p, device_id_type=MESH)
+    for copy in loads[:6]:
+        copy.wait()
 
     for i in range(GROUP):
         for h in range(2):
@@ -106,40 +116,22 @@
     wpad[...] = jnp.zeros_like(wpad)
     wpad[0:2, :] = wout[:, pl.ds(pl.multiple_of(m * COLS, COLS), COLS)].astype(F32)
 
-    pl.semaphore_wait(barrier, len(partners))
-
-    mine = pl.ds(pl.multiple_of(m * 16, 16), 16)
-    w0 = [send(wsrc.at[mm], w.at[:, yq, x, mine, :], to) for mm, to in members]
-    w[:, yq, x, mine, :] = wsrc[m]
-
-    for copy in loads:
-        copy.wait()
-    halo_src = own
-    halo_src[0] = edge[0, :, :, 0, :]
-    halo_src[1] = edge[1, :, :, 7, :]
-    halos = [
-        send(halo_src.at[0], halo_out.at[1], down_id),
-        send(halo_src.at[1], halo_out.at[0], up_id),
-    ]
-
     cnt = jnp.broadcast_to(counts[...].astype(F32), (16, TILES)).astype(BF)
     r_i, c_i = iota((TILES, TILES), 0), iota((TILES, TILES), 1)
     start = nt((c_i < r_i).astype(F32).astype(BF), cnt)[:, 0:1]
     ends = nt((c_i <= r_i).astype(F32).astype(BF), cnt)[:, 0:1]
+    start_row = nn(cnt, (r_i < c_i).astype(F32).astype(BF))[0:1].astype(jnp.int32)
     place = iota((TILES, PAD), 1).astype(F32)
     onehot = jnp.where((place >= start) & (place < ends), 1.0, 0.0).astype(BF)
     idx = index[...]
-    lane16 = iota((TILES, 16), 1)
-    table = jnp.zeros((TILES, 16), jnp.int32)
-    start_i = start.astype(jnp.int32)
-    pieces = []
-    for k in range(CAP):
-        col = idx[:, k:k + 1]
-        pieces += [(k, col >> 9), (4 + k, (col >> 4) & 31), (8 + k, col & 15)]
-    pieces += [(12, start_i >> 4), (13, start_i & 15), (14, routes[...])]
-    for at, col in pieces:
-        table = jnp.where(lane16 == at, col, table)
-    vals = tn(table.astype(F32).astype(BF), onehot)
+    table[...] = jnp.zeros_like(table)
+    table[0:4, :] = (idx >> 9).astype(F32)
+    table[4:8, :] = ((idx >> 4) & 31).astype(F32)
+    table[8:12, :] = (idx & 15).astype(F32)
+    table[12:13, :] = (start_row >> 4).astype(F32)
+    table[13:14, :] = (start_row & 15).astype(F32)
+    table[14:15, :] = routes[...].astype(F32)
+    vals = nn(table[...].astype(BF), onehot)
     lane = iota((1, PAD), 1)
     kk = lane.astype(F32) - (vals[12:13] * 16.0 + vals[13:14])
     zrow = jnp.zeros((1, PAD), F32)
@@ -156,6 +148,8 @@
     rowmeta[2:3, :] = jnp.where(valid, vals[14:15], -1.0)
     oz = jnp.where(iota((32, PAD), 0).astype(F32) == zrow, 1.0, 0.0)
     ox = jnp.where(iota((PAD, PAD), 0).astype(F32) == xrow, 1.0, 0.0).astype(BF)
+    for copy in loads[6:]:
+        copy.wait()
     tp = jnp.stack([tplanes[0, 1] - tplanes[0, 0], tplanes[1, 1] - tplanes[1, 0]])
     table_p = jnp.concatenate(
         [planes[...].reshape(384, PAD).astype(BF), tp.reshape(64, PAD).astype(BF)], axis=0
@@ -164,13 +158,17 @@
     picked = jnp.sum(got, axis=1)
     picked = jnp.concatenate([picked, jnp.zeros((2, PAD), F32)], axis=0)
     fbuf[m] = picked.astype(BF)
+
+    pl.semaphore_wait(barrier, len(partners))
+
+    mine = pl.ds(pl.multiple_of(m * 16, 16), 16)
+    w0 = [send(wsrc.at[mm], w.at[:, yq, x, mine, :], to) for mm, to in members]
+    w[:, yq, x, mine, :] = wsrc[m]
     fcopies = [send(fbuf.at[m], fbuf.at[m], to) for _, to in members]
-
     for copy in w0:
         copy.wait()
-    w1 = [send(w.at[0, yq, x], w.at[0, yq, x], to) for _, to in xs]
-    w1 += [send(w.at[1, yq, x], w.at[1, yq, x], to) for _, to in ys]
-
+    w1x = [send(w.at[:, yq, x], w.at[:, yq, x], to) for _, to in xs]
+    w1y = [send(w.at[:, yq, x], w.at[:, yq, x], to) for _, to in ys]
     for copy in fcopies:
         copy.wait()
     ftot[...] = jnp.zeros_like(ftot)
@@ -182,63 +180,82 @@
         ftot[:, 128 * base:128 * base + PAD + 128] += wide
     feats[...] = ftot[:, 0:S].astype(BF)
 
-    for copy in w1:
-        copy.wait()
-    w2 = [send(w.at[0, yq], w.at[0, yq], to) for _, to in ys]
-    w2 += [send(w.at[1, :, x], w.at[1, :, x], to) for _, to in xs]
+    w2 = []
+    for i, k in enumerate((1, 3, 2)):
+        w1x[i].wait()
+        xx = (x + 4 - k) % 4
+        w2 += [send(w.at[0, yq, xx], w.at[0, yq, xx], to) for _, to in ys]
+        w1y[i].wait()
+        yy = (y + 4 - k) % 4
+        qq = (yy % 2) * 2 + yy // 2
+        w2 += [send(w.at[1, qq, x], w.at[1, qq, x], to) for _, to in xs]
+    halos = [
+        send(own.at[0], halo_out.at[1], down_id),
+        send(own.at[1], halo_out.at[0], up_id),
+    ]
 
     def first(q):
-        sl = slice(CH * q, CH * q + CH)
+        at, size, slot = PARTS[q]
+        sl = slice(at, at + size)
 
         def inner(j, _):
             rows = pl.ds(pl.multiple_of(j * JT, JT), JT)
             act = jnp.tanh(nn(wint[rows, :], feats[:, sl]))
             t[rows, sl] = act
-            fs[rows, :] = act.astype(BF)
+            fs[rows, slot:slot + size] = act.astype(BF)
             return 0
 
         lax.fori_loop(0, H // JT, inner, 0, unroll=True)
 
-    for q in range(NCH):
-        sl = slice(CH * q, CH * q + CH)
-        first(q)
-        if q == 0:
-            for copy in w2:
-                copy.wait()
-            for h in range(2):
-                wct[128 * h:128 * h + 128, :] = w[h].reshape(H, 128).astype(F32).T.astype(BF)
-        act2 = jnp.tanh(nn(wct[...], fs[...]))
-        d2[:, sl] = 1.0 - act2 * act2
-        pbuf[m, 2 * q:2 * q + 2, :] = nn(wpad[...].astype(BF), act2.astype(BF))[0:2]
-    pbuf[m, 6:8, :] = jnp.zeros((2, CH), F32)
-    pcopies = [send(pbuf.at[m], pbuf.at[m], to) for _, to in members]
-    for copy in pcopies:
-        copy.wait()
-
-    total = pbuf[0]
-    for i in range(1, GROUP):
-        total = total + pbuf[i]
-    pred = jnp.concatenate([total[2 * q:2 * q + 2] for q in range(NCH)], axis=1)
-    err = pred - ftot[12:14, 0:S]
-    perr[0:2, :] = pred
-    perr[2:4, :] = err
+    pcopies = []
+
+    def second(q):
+        at, size, slot = PARTS[q]
+        act2 = jnp.tanh(nn(wct[...], fs[:, slot:slot + size]))
+        d2[:, at:at + size] = 1.0 - act2 * act2
+        pbuf[m, q, :, 0:size] = nn(wpad[...].astype(BF), act2.astype(BF))[0:2]
+        ref = pbuf.at[m, q, :, 0:size]
+        pcopies.append([send(ref, ref, to) for _, to in members])
+
+    first(0)
+    first(1)
+    for copy in w2:
+        copy.wait()
+    for h in range(2):
+        wct[128 * h:128 * h + 128, :] = w[h].reshape(H, 128).astype(F32).T.astype(BF)
+    second(0)
+    first(2)
+    second(1)
+    first(3)
+    second(2)
+    second(3)
     perr[4:8, :] = jnp.zeros((4, S), F32)
-    bo = (perr[...] * SCALE)
-    bo = jnp.concatenate([bo[2:4], jnp.zeros((14, S), F32)], axis=0).astype(BF)
-    for q in range(NCH):
-        sl = slice(CH * q, CH * q + CH)
-        bst[:, sl] = (tn(wpad[...].astype(BF), bo[:, sl]) * d2[:, sl]).astype(BF)
-
-    def mid(q, _):
+    for q, (at, size, _) in enumerate(PARTS):
+        sl = slice(at, at + size)
+        for copy in pcopies[q]:
+            copy.wait()
+        pred = pbuf[0, q, :, 0:size]
+        for i in range(1, GROUP):
+            pred = pred + pbuf[i, q, :, 0:size]
+        err = pred - ftot[12:14, sl]
+        perr[0:2, sl] = pred
+        perr[2:4, sl] = err
+        bo = jnp.concatenate([err * SCALE, jnp.zeros((14, size), F32)], axis=0).astype(BF)
+        bst[:, sl] = (tn(wpad[...].astype(BF), bo) * d2[:, sl]).astype(BF)
+
+    s1a = []
+    s1b = []
+    for n, k in enumerate((1, 3, 2, 0)):
+        yy = (y + k) % 4
+        q = (yy % 2) * 2 + yy // 2
         rows = pl.ds(pl.multiple_of(q * JT, JT), JT)
         part = nt(t[rows, :].astype(BF), bst[...])
         for h in range(2):
             gm[h, q] = part[:, 128 * h:128 * h + 128].reshape(4, 128, 128)
-        return 0
-
-    lax.fori_loop(0, H // JT, mid, 0)
-    s1 = [send(gm.at[0, :, xx], ra.at[i], to) for i, (xx, to) in enumerate(xs)]
-    s1 += [send(gm.at[1, yy], rb.at[i], to) for i, (yy, to) in enumerate(ys)]
+        if k:
+            s1b.append(send(gm.at[1, q], rb.at[n], ys[n][1]))
+        for i, (xx, to) in enumerate(xs):
+            s1a.append(send(gm.at[0, q, xx], ra.at[i, q], to))
 
     rolled = pltpu.roll(perr[...], (S - LIVE * m) % S, 1)[:, 0:PAD]
     meta_out[0:2, :] = jnp.where(valid, rolled[0:2], 0.0)
@@ -273,12 +290,12 @@
         send(gwp.at[:, pl.ds(pl.multiple_of(mm * COLS, COLS), COLS)], rg.at[i], to)
         for i, (mm, to) in enumerate(members)
     ]
-    for copy in s1:
-        copy.wait()
-    acc_a[...] = gm[0, :, x] + ra[0] + ra[1] + ra[2]
-    acc_b[...] = gm[1, yq] + rb[0] + rb[1] + rb[2]
-    s2 = [send(acc_a.at[yy], r2a.at[i], to) for i, (yy, to) in enumerate(ys)]
-    s2 += [send(acc_b.at[xx], r2b.at[i], to) for i, (xx, to) in enumerate(xs)]
+    for copy in s1a + s1b:
+        copy.wait()
+    gm[0, :, x] = gm[0, :, x] + ra[0] + ra[1] + ra[2]
+    gm[1, yq] = gm[1, yq] + rb[0] + rb[1] + rb[2]
+    s2 = [send(gm.at[0, yy, x], r2a.at[i], to) for i, (yy, to) in enumerate(ys)]
+    s2 += [send(gm.at[1, yq, xx], r2b.at[i], to) for i, (xx, to) in enumerate(xs)]
 
     my_cols = pl.ds(pl.multiple_of(m * COLS, COLS), COLS)
     for copy in g1:
@@ -286,32 +303,31 @@
     part = gwp[:, my_cols]
     for i in range(7):
         part = part + rg[i]
-    rgx[x] = part
-    g2 = [send(rgx.at[x], rgx.at[x], to) for _, to in xs]
-    for copy in g2:
-        copy.wait()
-    rgy[yq] = (rgx[0] + rgx[1]) + (rgx[2] + rgx[3])
-    g3 = [send(rgy.at[yq], rgy.at[yq], to) for _, to in ys]
+    rgp[yq * 4 + x] = part
+    g2 = [send(rgp.at[yq * 4 + x], rgp.at[yq * 4 + x], to) for to in plane]
 
     for copy in s2:
         copy.wait()
-    fin[0] = acc_a[yq] + r2a[0] + r2a[1] + r2a[2]
-    fin[1] = acc_b[x] + r2b[0] + r2b[1] + r2b[2]
+    fin[0] = gm[0, yq, x] + r2a[0] + r2a[1] + r2a[2]
+    fin[1] = gm[1, yq, x] + r2b[0] + r2b[1] + r2b[2]
     s3 = [
         send(fin.at[:, pl.ds(pl.multiple_of(mm * 16, 16), 16), :], gmid_out.at[m], to)
         for mm, to in members
     ]
     gmid_out[m] = fin[:, mine, :]
 
-    for copy in g3:
-        copy.wait()
-    small_out[m] = (rgy[0] + rgy[1]) + (rgy[2] + rgy[3])
+    for copy in g2:
+        copy.wait()
+    part = rgp[0]
+    for i in range(1, 16):
+        part = part + rgp[i]
+    small_out[m] = part
     g4 = [send(small_out.at[m], small_out.at[m], to) for _, to in members]
     for copy in s3 + g4 + halos:
         copy.wait()
 
 
-N_SENDS = 7 + 2 + 7 + 6 + 6 + 7 + 6 + 7 + 6 + 3 + 3 + 7 + 7
+N_SENDS = 7 + 7 + 6 + 18 + 2 + 28 + 12 + 3 + 6 + 7 + 7 + 15 + 7
 
 
 def train(flow, counts, routes, index, win, wmid, wout):
@@ -325,11 +341,11 @@
             sds((GROUP, 16, COLS), F32),
             sds((GROUP, 2, 16, 128), F32),
         ),
-        in_specs=[pl.BlockSpec(memory_space=pl.ANY)] + [vm] * 6,
-        out_specs=(vm,) * 4,
+        in_specs=[pl.BlockSpec(memory_space=pl.ANY)] * 7,
+        out_specs=(pl.BlockSpec(memory_space=pl.ANY), vm, vm, vm),
         scratch_shapes=[
             pltpu.VMEM((H, S), F32),
-            pltpu.VMEM((H, CH), BF),
+            pltpu.VMEM((H, 1920), BF),
             pltpu.VMEM((2, 4, 4, 128, 128), BF),
             pltpu.VMEM((COLS, H), BF),
             pltpu.VMEM((COLS, S), F32),
@@ -337,14 +353,11 @@
             pltpu.VMEM((2, 4, 4, 128, 128), F32),
             pltpu.VMEM((3, 4, 128, 128), F32),
             pltpu.VMEM((3, 4, 128, 128), F32),
-            pltpu.VMEM((4, 128, 128), F32),
-            pltpu.VMEM((4, 128, 128), F32),
             pltpu.VMEM((3, 128, 128), F32),
             pltpu.VMEM((3, 128, 128), F32),
             pltpu.VMEM((2, 128, 128), F32),
             pltpu.VMEM((4, 3, 32, 512), F32),
             pltpu.VMEM((2, 2, 32, 512), F32),
-            pltpu.VMEM((2, 5, 8, 8, 512), F32),
             pltpu.VMEM((GROUP, 2, 16, 128), BF),
             pltpu.VMEM((H, 16), BF),
             pltpu.VMEM((16, COLS), F32),
@@ -352,14 +365,20 @@
             pltpu.VMEM((GROUP, 16, PAD), BF),
             pltpu.VMEM((16, S + 128), F32),
             pltpu.VMEM((16, S), BF),
-            pltpu.VMEM((GROUP, 8, CH), F32),
+            pltpu.VMEM((GROUP, len(PARTS), 2, CH), F32),
             pltpu.VMEM((8, PAD), F32),
             pltpu.VMEM((8, S), F32),
             pltpu.VMEM((16, H), F32),
             pltpu.VMEM((7, 16, COLS), F32),
-            pltpu.VMEM((4, 16, COLS), F32),
-            pltpu.VMEM((4, 16, COLS), F32),
-            pltpu.SemaphoreType.DMA((5,)),
+            pltpu.VMEM((16, 16, COLS), F32),
+            pltpu.VMEM((1, TILES), jnp.int32),
+            pltpu.VMEM((1, TILES), jnp.int32),
+            pltpu.VMEM((CAP, TILES), jnp.int32),
+            pltpu.VMEM((12, H), BF),
+            pltpu.VMEM((16, H), BF),
+            pltpu.VMEM((2, H), BF),
+            pltpu.VMEM((16, TILES), F32),
+            pltpu.SemaphoreType.DMA((11,)),
             pltpu.SemaphoreType.DMA((N_SENDS,)),
             pltpu.SemaphoreType.DMA((N_SENDS,)),
         ],
@@ -367,7 +386,7 @@
             collective_id=0, has_side_effects=True, vmem_limit_bytes=62 * 2**20
         ),
         name="train",
-    )(flow, counts, routes, index, win, wmid, wout)
+    )(flow, counts, routes.reshape(1, TILES), index.T, win, wmid, wout)
 
 
 def slab_kernel(flow, diff, stress, halo, meta, small, gmid, field, new_stress, loss, gw, gwm):
@@ -437,7 +456,7 @@
             block, whole((2, 32, 512)), pl.BlockSpec(memory_space=pltpu.SMEM),
             whole((12, H)), whole((16, H)),
         ),
-        compiler_params=pltpu.CompilerParams(vmem_limit_bytes=32 * 2**20),
+        compiler_params=pltpu.CompilerParams(vmem_limit_bytes=62 * 2**20),
         name="slab",
     )(flow, diff, stress, halo, meta, small, gmid)
 

time: 89.3 us -> 78.4 us (0.88)
  local copies, waits for them, and re-layouts: 8.14 us -> 0 us
  Pallas kernels: 80 us -> 77.3 us
    unnamed x16 -> x0, local copies, waits for them, and re-layouts: 8.14 us -> none
    pallas_call x1, Pallas kernels: 75.6 us -> 70.6 us  [train(): pl.pallas_call(train_kernel, out_shape=(sds((2, 5, 8, 512), F32), sds((8,...]
    pallas_call x1, Pallas kernels: 4.36 us -> 6.7 us  [slab(): pl.pallas_call(slab_kernel, grid=(5,), out_shape=(sds((5, 8, 32, 512), F3...]
where the time goes in v2:
time: 78.4 us; the launch traced here: 78.1 us
  Pallas kernels  77.3 us (99%)
  between operations  0.8 us (1%)
    pallas_call x1, Pallas kernels, train(): pl.pallas_call(train_kernel, out_shape=(sds((2, 5, 8, 512), F32), sds((8,...  70.6 us
    pallas_call x1, Pallas kernels, slab(): pl.pallas_call(slab_kernel, grid=(5,), out_shape=(sds((5, 8, 32, 512), F3...  6.7 us

profile of v2, /device:TPU:1, one launch (start us, length us, event | category | flops | bytes accessed | tf_op | source)
XLA Modules:
  0.0 78.1 jit_solution(4942707548375092307)
XLA Ops:
  0.6 70.6 %train.1 = (f32[2,5,8,512]{3,2,1,0:T(8,128)}, f32[8,512]{1,0:T(8,128)}, f32[8,16,256]{2,1,0:T(8,128)}, f32[8,2,16,128]{3,2,1,0:T(8,128)}) custom-call(f32[5,8,32,512]{3,2,1,0:T(8,128)} %flow.3, s32[1,192]{1,0:T(1,128)} %counts_h.1, s32[1,192]{1,0:T(1,128)} %bitcast.3, s32[4,192]{1,0:T(4,128)} %bitcast.2, bf16[12,2048]{1,0:T(8,128)(2,1)} %win_h.1, ...), custom_call_target="tpu_custom_call" | custom-call | tf_op jit(solution)/shard_map/train/pallas_call | solution.py:336
  71.3 6.7 %slab.1 = (f32[5,8,32,512]{3,2,1,0:T(8,128)}, f32[2,32,512]{2,1,0:T(8,128)}, f32[1]{0:T(128)}, f32[12,2048]{1,0:T(8,128)}, f32[16,2048]{1,0:T(8,128)}) custom-call(f32[5,8,32,512]{3,2,1,0:T(8,128)} %flow.3, f32[8,32,512]{2,1,0:T(8,128)} %diff.1, f32[2,32,512]{2,1,0:T(8,128)} %stress.1, f32[2,5,8,512]{3,2,1,0:T(8,128)} %get-tuple-element.9.halo, ...), custom_call_target="tpu_custom_call" | custom-call | tf_op jit(solution)/shard_map/slab/pallas_call | solution.py:441

commit v3 on v2

--- a/solution.py
+++ b/solution.py
@@ -46,11 +46,11 @@
 
 
 def train_kernel(
-    flow, counts_h, routes_h, index_h, win_h, wmid_h, wout_h,
-    halo_out, meta_out, small_out, gmid_out,
+    flow, flat_flow, diff_h, counts_h, routes_h, index_h, win_h, wmid_h, wout_h,
+    adv_out, meta_out, small_out, gmid_out,
     t, fs, w, wct, d2, bst, gm, ra, rb, r2a, r2b, fin,
-    planes, tplanes, wsrc, wint, wpad, own, fbuf, ftot, feats, pbuf, rowmeta, perr,
-    gwp, rg, rgp, counts, routes, index, win, wmid, wout, table,
+    planes, tplanes, halo, wsrc, wint, wpad, own, fbuf, ftot, feats, pbuf, rowmeta, perr,
+    gwp, rg, rgp, counts, routes, index, win, wmid, wout, table, metav, smallv,
     lsem, ssem, rsem,
 ):
     sec = lax.axis_index("sec")
@@ -96,8 +96,8 @@
         pl.semaphore_signal(barrier, inc=1, device_id=p, device_id_type=MESH)
 
     pairs = [
-        (counts_h, counts), (routes_h, routes), (index_h, index), (win_h, win),
-        (wout_h, wout), (wmid_h, wmid),
+        (wmid_h, wmid), (counts_h, counts), (routes_h, routes), (index_h, index),
+        (win_h, win), (wout_h, wout),
         (flow.at[0:4, 0:3], planes), (flow.at[1, 3:5], tplanes.at[0]),
         (flow.at[3, 3:5], tplanes.at[1]), (flow.at[:, :, 0, :], own.at[0]),
         (flow.at[:, :, 31, :], own.at[1]),
@@ -105,12 +105,13 @@
     loads = [pltpu.make_async_copy(a, b, lsem.at[i]) for i, (a, b) in enumerate(pairs)]
     for copy in loads:
         copy.start()
-    for copy in loads[:6]:
-        copy.wait()
+    loads[0].wait()
 
     for i in range(GROUP):
         for h in range(2):
             wsrc[i, h] = wmid[:, COLS * i + 128 * h:COLS * i + 128 * h + 128]
+    for copy in loads[1:6]:
+        copy.wait()
     winp = jnp.concatenate([win[...].astype(F32), jnp.zeros((4, H), F32)], axis=0)
     wint[...] = winp.T.astype(BF)
     wpad[...] = jnp.zeros_like(wpad)
@@ -190,8 +191,8 @@
         qq = (yy % 2) * 2 + yy // 2
         w2 += [send(w.at[1, qq, x], w.at[1, qq, x], to) for _, to in xs]
     halos = [
-        send(own.at[0], halo_out.at[1], down_id),
-        send(own.at[1], halo_out.at[0], up_id),
+        send(own.at[0], halo.at[1], down_id),
+        send(own.at[1], halo.at[0], up_id),
     ]
 
     def first(q):
@@ -258,9 +259,11 @@
             s1a.append(send(gm.at[0, q, xx], ra.at[i, q], to))
 
     rolled = pltpu.roll(perr[...], (S - LIVE * m) % S, 1)[:, 0:PAD]
-    meta_out[0:2, :] = jnp.where(valid, rolled[0:2], 0.0)
-    meta_out[2:4, :] = rowmeta[0:2, :]
-    meta_out[4:8, :] = jnp.zeros((4, PAD), F32)
+    metav[0:2, :] = jnp.where(valid, rolled[0:2], 0.0)
+    metav[2:4, :] = rowmeta[0:2, :]
+    metav[4:8, :] = jnp.zeros((4, PAD), F32)
+    stores = [pltpu.make_async_copy(metav, meta_out, lsem.at[18])]
+    stores[0].start()
     square = rolled[2:3] * rolled[2:3] + rolled[3:4] * rolled[3:4]
     square = jnp.where(valid, square, 0.0)
     chosen = iota((DEVICES, PAD), 0).astype(F32) == rowmeta[2:3, :]
@@ -281,23 +284,52 @@
         gwp[:, rows] = acc
         return 0
 
-    lax.fori_loop(0, H // JT, back, 0)
+    lax.fori_loop(0, H // JT - 1, back, 0)
+    slab_loads = [
+        pltpu.make_async_copy(flat_flow, t.at[0:1280, 0:512], lsem.at[11]),
+        pltpu.make_async_copy(diff_h, t.at[0:256, 512:1024], lsem.at[12]),
+    ]
+    for copy in slab_loads:
+        copy.start()
+    back(H // JT - 1, 0)
     gwp[12:16, :] = jnp.zeros((4, H), F32)
     gwp[12:13, 0:DEVICES] = loss_row
     gwp[13:14, 0:DEVICES] = count_row
 
+    def stencil(v):
+        row, col = iota((32, 512), 0), iota((32, 512), 1)
+        for l in range(8):
+            at = v * 256 + l * 32
+            u = t[at:at + 32, 0:512]
+            low, high = halo[0, v, l:l + 1, :], halo[1, v, l:l + 1, :]
+            below_z = jnp.where(row == 0, low, pltpu.roll(u, 1, 0))
+            above_z = jnp.where(row == 31, high, pltpu.roll(u, 31, 0))
+            below_x = jnp.where(col == 0, u, pltpu.roll(u, 1, 1))
+            above_x = jnp.where(col == 511, u, pltpu.roll(u, 511, 1))
+            below_y = t[at - 32:at, 0:512] if l > 0 else u
+            above_y = t[at + 32:at + 64, 0:512] if l < 7 else u
+            spread = below_x + above_x + below_y + above_y + below_z + above_z - 6.0 * u
+            value = u + ADVECT * (below_x - u) + t[l * 32:l * 32 + 32, 512:1024] * spread
+            t[at:at + 32, 1024:1536] = value
+        rows = slice(v * 256, v * 256 + 256)
+        copy = pltpu.make_async_copy(t.at[rows, 1024:1536], adv_out.at[rows, :], lsem.at[13 + v])
+        copy.start()
+        stores.append(copy)
+
     g1 = [
         send(gwp.at[:, pl.ds(pl.multiple_of(mm * COLS, COLS), COLS)], rg.at[i], to)
         for i, (mm, to) in enumerate(members)
     ]
-    for copy in s1a + s1b:
+    for copy in s1a + s1b + halos + slab_loads:
         copy.wait()
     gm[0, :, x] = gm[0, :, x] + ra[0] + ra[1] + ra[2]
     gm[1, yq] = gm[1, yq] + rb[0] + rb[1] + rb[2]
     s2 = [send(gm.at[0, yy, x], r2a.at[i], to) for i, (yy, to) in enumerate(ys)]
     s2 += [send(gm.at[1, yq, xx], r2b.at[i], to) for i, (xx, to) in enumerate(xs)]
 
+    stencil(0)
     my_cols = pl.ds(pl.multiple_of(m * COLS, COLS), COLS)
+    stencil(1)
     for copy in g1:
         copy.wait()
     part = gwp[:, my_cols]
@@ -306,6 +338,7 @@
     rgp[yq * 4 + x] = part
     g2 = [send(rgp.at[yq * 4 + x], rgp.at[yq * 4 + x], to) for to in plane]
 
+    stencil(2)
     for copy in s2:
         copy.wait()
     fin[0] = gm[0, yq, x] + r2a[0] + r2a[1] + r2a[2]
@@ -314,35 +347,39 @@
         send(fin.at[:, pl.ds(pl.multiple_of(mm * 16, 16), 16), :], gmid_out.at[m], to)
         for mm, to in members
     ]
-    gmid_out[m] = fin[:, mine, :]
+    stores.append(pltpu.make_async_copy(fin.at[:, mine, :], gmid_out.at[m], lsem.at[19]))
+    stores[-1].start()
+    stencil(3)
 
     for copy in g2:
         copy.wait()
     part = rgp[0]
     for i in range(1, 16):
         part = part + rgp[i]
-    small_out[m] = part
-    g4 = [send(small_out.at[m], small_out.at[m], to) for _, to in members]
-    for copy in s3 + g4 + halos:
+    smallv[...] = part
+    g4 = [send(smallv, small_out.at[m], to) for _, to in members]
+    stores.append(pltpu.make_async_copy(smallv, small_out.at[m], lsem.at[20]))
+    stores[-1].start()
+    stencil(4)
+    for copy in s3 + g4 + stores:
         copy.wait()
 
 
 N_SENDS = 7 + 7 + 6 + 18 + 2 + 28 + 12 + 3 + 6 + 7 + 7 + 15 + 7
 
 
-def train(flow, counts, routes, index, win, wmid, wout):
-    vm = pl.BlockSpec(memory_space=pltpu.VMEM)
+def train(flow, diff, counts, routes, index, win, wmid, wout):
     sds = jax.ShapeDtypeStruct
     return pl.pallas_call(
         train_kernel,
         out_shape=(
-            sds((2, 5, 8, 512), F32),
+            sds((1280, 512), F32),
             sds((8, PAD), F32),
             sds((GROUP, 16, COLS), F32),
             sds((GROUP, 2, 16, 128), F32),
         ),
-        in_specs=[pl.BlockSpec(memory_space=pl.ANY)] * 7,
-        out_specs=(pl.BlockSpec(memory_space=pl.ANY), vm, vm, vm),
+        in_specs=[pl.BlockSpec(memory_space=pl.ANY)] * 9,
+        out_specs=(pl.BlockSpec(memory_space=pl.ANY),) * 4,
         scratch_shapes=[
             pltpu.VMEM((H, S), F32),
             pltpu.VMEM((H, 1920), BF),
@@ -358,6 +395,7 @@
             pltpu.VMEM((2, 128, 128), F32),
             pltpu.VMEM((4, 3, 32, 512), F32),
             pltpu.VMEM((2, 2, 32, 512), F32),
+            pltpu.VMEM((2, 5, 8, 512), F32),
             pltpu.VMEM((GROUP, 2, 16, 128), BF),
             pltpu.VMEM((H, 16), BF),
             pltpu.VMEM((16, COLS), F32),
@@ -378,7 +416,9 @@
             pltpu.VMEM((16, H), BF),
             pltpu.VMEM((2, H), BF),
             pltpu.VMEM((16, TILES), F32),
-            pltpu.SemaphoreType.DMA((11,)),
+            pltpu.VMEM((8, PAD), F32),
+            pltpu.VMEM((16, COLS), F32),
+            pltpu.SemaphoreType.DMA((21,)),
             pltpu.SemaphoreType.DMA((N_SENDS,)),
             pltpu.SemaphoreType.DMA((N_SENDS,)),
         ],
@@ -386,61 +426,70 @@
             collective_id=0, has_side_effects=True, vmem_limit_bytes=62 * 2**20
         ),
         name="train",
-    )(flow, counts, routes.reshape(1, TILES), index.T, win, wmid, wout)
-
-
-def slab_kernel(flow, diff, stress, halo, meta, small, gmid, field, new_stress, loss, gw, gwm):
-    v = pl.program_id(0)
-
-    @pl.when(v == 0)
-    def _():
-        zrow, xrow = meta[2:3, :], meta[3:4, :]
-        oz = jnp.where(iota((32, PAD), 0).astype(F32) == zrow, 1.0, 0.0)
-        ox = jnp.where(iota((PAD, PAD), 0).astype(F32) == xrow, 1.0, 0.0).astype(BF)
-        lhs = jnp.concatenate([oz * meta[0:1, :], oz * meta[1:2, :], oz], axis=0).astype(BF)
-        spread = nt(lhs, ox)
-        hit = spread[64:96] > 0.5
-        new_stress[0] = jnp.where(hit, spread[0:32], stress[0])
-        new_stress[1] = jnp.where(hit, spread[32:64], stress[1])
-        me = lax.axis_index("sec") * 64 + lax.axis_index("dev")
-        ratio = 0.5 * small[0, 12:13, 0:DEVICES] / small[0, 13:14, 0:DEVICES]
-        loss[0] = jnp.sum(jnp.where(iota((1, DEVICES), 1) == me, ratio, 0.0))
-        for i in range(GROUP):
-            gw[:, COLS * i:COLS * i + COLS] = small[i, 0:12, :]
-            for h in range(2):
-                at = COLS * i + 128 * h
-                gwm[:, at:at + 128] = gmid[i, h]
-
-    u = flow[0]
-    row, col = iota((8, 32, 512), 1), iota((8, 32, 512), 2)
-    below_z = jnp.where(row == 0, halo[0, v][:, None, :], pltpu.roll(u, 1, 1))
-    above_z = jnp.where(row == 31, halo[1, v][:, None, :], pltpu.roll(u, 31, 1))
-    below_x = jnp.where(col == 0, u, pltpu.roll(u, 1, 2))
-    above_x = jnp.where(col == 511, u, pltpu.roll(u, 511, 2))
-    below_y = jnp.concatenate([u[0:1], u[0:7]], axis=0)
-    above_y = jnp.concatenate([u[1:8], u[7:8]], axis=0)
-    spread = below_x + above_x + below_y + above_y + below_z + above_z - 6.0 * u
-    field[0] = u + ADVECT * (below_x - u) + diff[...] * spread
-
-    @pl.when(v == 1)
-    def _():
-        field[0, 0] = field[0, 0] - GAIN * new_stress[0]
-
-    @pl.when(v == 3)
-    def _():
-        field[0, 0] = field[0, 0] - GAIN * new_stress[1]
-
-
-def slab(flow, diff, stress, halo, meta, small, gmid):
+    )(flow, flow.reshape(1280, 512), diff.reshape(256, 512), counts, routes.reshape(1, TILES), index.T, win, wmid, wout)
+
+
+def finish_kernel(
+    adv, stress_h, meta_h, small_h, gmid_h, field, new_stress, loss, gw, gwm,
+    held, stress, meta, small, gmid, wall, gwv, gwmv, sem,
+):
+    order = (1, 3, 0, 2, 4)
+    first = [
+        pltpu.make_async_copy(meta_h, meta, sem.at[10]),
+        pltpu.make_async_copy(stress_h, stress, sem.at[11]),
+    ]
+    then = [
+        pltpu.make_async_copy(small_h, small, sem.at[12]),
+        pltpu.make_async_copy(gmid_h, gmid, sem.at[13]),
+    ]
+    loads = {v: pltpu.make_async_copy(adv.at[v], held.at[v], sem.at[v]) for v in order}
+    stores = {v: pltpu.make_async_copy(held.at[v], field.at[v], sem.at[5 + v]) for v in order}
+    last = [
+        pltpu.make_async_copy(wall, new_stress, sem.at[14]),
+        pltpu.make_async_copy(gwv, gw, sem.at[15]),
+        pltpu.make_async_copy(gwmv, gwm, sem.at[16]),
+    ]
+    for copy in first + [loads[v] for v in order] + then:
+        copy.start()
+    first[0].wait()
+    zrow, xrow = meta[2:3, :], meta[3:4, :]
+    oz = jnp.where(iota((32, PAD), 0).astype(F32) == zrow, 1.0, 0.0)
+    ox = jnp.where(iota((PAD, PAD), 0).astype(F32) == xrow, 1.0, 0.0).astype(BF)
+    lhs = jnp.concatenate([oz * meta[0:1, :], oz * meta[1:2, :], oz], axis=0).astype(BF)
+    spread = nt(lhs, ox)
+    hit = spread[64:96] > 0.5
+    first[1].wait()
+    for v in (0, 2, 4):
+        loads[v].wait()
+        stores[v].start()
+    for i, v in enumerate((1, 3)):
+        value = jnp.where(hit, spread[32 * i:32 * i + 32], stress[i])
+        wall[i] = value
+        loads[v].wait()
+        held[v, 0] = held[v, 0] - GAIN * value
+        stores[v].start()
+    last[0].start()
+    for copy in then:
+        copy.wait()
+    for i in range(GROUP):
+        gwv[:, COLS * i:COLS * i + COLS] = small[i, 0:12, :]
+        for h in range(2):
+            at = COLS * i + 128 * h
+            gwmv[:, at:at + 128] = gmid[i, h]
+    last[1].start()
+    last[2].start()
+    me = lax.axis_index("sec") * 64 + lax.axis_index("dev")
+    ratio = 0.5 * small[0, 12:13, 0:DEVICES] / small[0, 13:14, 0:DEVICES]
+    loss[0] = jnp.sum(jnp.where(iota((1, DEVICES), 1) == me, ratio, 0.0))
+    for copy in [stores[v] for v in order] + last:
+        copy.wait()
+
+
+def finish(adv, stress, meta, small, gmid):
     sds = jax.ShapeDtypeStruct
-
-    def whole(shape):
-        return pl.BlockSpec(shape, lambda v: (0,) * len(shape))
-
-    block = pl.BlockSpec((1, 8, 32, 512), lambda v: (v, 0, 0, 0))
+    anywhere = pl.BlockSpec(memory_space=pl.ANY)
     return pl.pallas_call(
-        slab_kernel,
-        grid=(5,),
+        finish_kernel,
         out_shape=(
             sds((5, 8, 32, 512), F32),
             sds((2, 32, 512), F32),
@@ -448,22 +497,27 @@
             sds((12, H), F32),
             sds((16, H), F32),
         ),
-        in_specs=[
-            block, whole((8, 32, 512)), whole((2, 32, 512)), whole((2, 5, 8, 512)),
-            whole((8, PAD)), whole((GROUP, 16, COLS)), whole((GROUP, 2, 16, 128)),
+        in_specs=[anywhere] * 5,
+        out_specs=(anywhere, anywhere, pl.BlockSpec(memory_space=pltpu.SMEM), anywhere, anywhere),
+        scratch_shapes=[
+            pltpu.VMEM((5, 8, 32, 512), F32),
+            pltpu.VMEM((2, 32, 512), F32),
+            pltpu.VMEM((8, PAD), F32),
+            pltpu.VMEM((GROUP, 16, COLS), F32),
+            pltpu.VMEM((GROUP, 2, 16, 128), F32),
+            pltpu.VMEM((2, 32, 512), F32),
+            pltpu.VMEM((12, H), F32),
+            pltpu.VMEM((16, H), F32),
+            pltpu.SemaphoreType.DMA((17,)),
         ],
-        out_specs=(
-            block, whole((2, 32, 512)), pl.BlockSpec(memory_space=pltpu.SMEM),
-            whole((12, H)), whole((16, H)),
-        ),
         compiler_params=pltpu.CompilerParams(vmem_limit_bytes=62 * 2**20),
-        name="slab",
-    )(flow, diff, stress, halo, meta, small, gmid)
+        name="finish",
+    )(adv.reshape(5, 8, 32, 512), stress, meta, small, gmid)
 
 
 def body(flow, diff, stress, counts, routes, index, win, wmid, wout):
-    halo, meta, small, gmid = train(flow, counts, routes, index, win, wmid, wout)
-    return slab(flow, diff, stress, halo, meta, small, gmid)
+    adv, meta, small, gmid = train(flow, diff, counts, routes, index, win, wmid, wout)
+    return finish(adv, stress, meta, small, gmid)
 
 
 def solution(mesh):

time: 78.4 us -> 74.7 us (0.953)
  Pallas kernels: 77.3 us -> 73.8 us
    pallas_call x2, Pallas kernels: 77.3 us -> 73.8 us  [the longest x1 70.1 us: train(): pl.pallas_call(train_kernel, out_shape=(sds((1280, 512), F32), sds((8, PA...]
where the time goes in v3:
time: 74.7 us; the launch traced here: 74.6 us
  Pallas kernels  73.8 us (99%)
  between operations  0.8 us (1%)
    pallas_call x1, Pallas kernels, train(): pl.pallas_call(train_kernel, out_shape=(sds((1280, 512), F32), sds((8, PA...  70.1 us
    pallas_call x1, Pallas kernels, finish(): pl.pallas_call(finish_kernel, out_shape=(sds((5, 8, 32, 512), F32), sds((...  3.71 us

profile of v3, /device:TPU:1, one launch (start us, length us, event | category | flops | bytes accessed | tf_op | source)
XLA Modules:
  0.0 74.6 jit_solution(13768300597884440931)
XLA Ops:
  0.6 70.1 %train.1 = (f32[1280,512]{1,0:T(8,128)}, f32[8,512]{1,0:T(8,128)}, f32[8,16,256]{2,1,0:T(8,128)}, f32[8,2,16,128]{3,2,1,0:T(8,128)}) custom-call(f32[5,8,32,512]{3,2,1,0:T(8,128)} %flow.1, f32[1280,512]{1,0:T(8,128)} %bitcast.5, f32[256,512]{1,0:T(8,128)} %bitcast.7, s32[1,192]{1,0:T(1,128)} %counts_h.1, s32[1,192]{1,0:T(1,128)} %bitcast.9, ...), custom_call_target="tpu_custom_call" | custom-call | tf_op jit(solution)/shard_map/train/pallas_call | solution.py:373
  70.7 3.7 %finish.1 = (f32[5,8,32,512]{3,2,1,0:T(8,128)}, f32[2,32,512]{2,1,0:T(8,128)}, f32[1]{0:T(128)}, f32[12,2048]{1,0:T(8,128)}, f32[16,2048]{1,0:T(8,128)}) custom-call(f32[5,8,32,512]{3,2,1,0:T(8,128)} %bitcast.6, f32[2,32,512]{2,1,0:T(8,128)} %stress_h.1, f32[8,512]{1,0:T(8,128)} %get-tuple-element.10.meta_h, f32[8,16,256]{2,1,0:T(8,128)} %get-tuple-element.11.small_h, ...), custom_call_target="tpu_custom_call" | custom-call | tf_op jit(solution)/shard_map/finish/pallas_call | solution.py:491

commit v4 on v3

--- a/solution.py
+++ b/solution.py
@@ -112,10 +112,6 @@
             wsrc[i, h] = wmid[:, COLS * i + 128 * h:COLS * i + 128 * h + 128]
     for copy in loads[1:6]:
         copy.wait()
-    winp = jnp.concatenate([win[...].astype(F32), jnp.zeros((4, H), F32)], axis=0)
-    wint[...] = winp.T.astype(BF)
-    wpad[...] = jnp.zeros_like(wpad)
-    wpad[0:2, :] = wout[:, pl.ds(pl.multiple_of(m * COLS, COLS), COLS)].astype(F32)
 
     cnt = jnp.broadcast_to(counts[...].astype(F32), (16, TILES)).astype(BF)
     r_i, c_i = iota((TILES, TILES), 0), iota((TILES, TILES), 1)
@@ -166,6 +162,10 @@
     w0 = [send(wsrc.at[mm], w.at[:, yq, x, mine, :], to) for mm, to in members]
     w[:, yq, x, mine, :] = wsrc[m]
     fcopies = [send(fbuf.at[m], fbuf.at[m], to) for _, to in members]
+    winp = jnp.concatenate([win[...].astype(F32), jnp.zeros((4, H), F32)], axis=0)
+    wint[...] = winp.T.astype(BF)
+    wpad[...] = jnp.zeros_like(wpad)
+    wpad[0:2, :] = wout[:, pl.ds(pl.multiple_of(m * COLS, COLS), COLS)].astype(F32)
     for copy in w0:
         copy.wait()
     w1x = [send(w.at[:, yq, x], w.at[:, yq, x], to) for _, to in xs]

time: 74.7 us -> 74.8 us (level)
  no operation moved by 1% of the time
where the time goes in v4:
time: 74.8 us; the launch traced here: 74.6 us
  Pallas kernels  73.8 us (99%)
  between operations  0.8 us (1%)
    pallas_call x1, Pallas kernels, train(): pl.pallas_call(train_kernel, out_shape=(sds((1280, 512), F32), sds((8, PA...  70.1 us
    pallas_call x1, Pallas kernels, finish(): pl.pallas_call(finish_kernel, out_shape=(sds((5, 8, 32, 512), F32), sds((...  3.71 us

profile of v4, /device:TPU:1, one launch (start us, length us, event | category | flops | bytes accessed | tf_op | source)
XLA Modules:
  0.0 74.6 jit_solution(1891860586549788521)
XLA Ops:
  0.6 70.1 %train.1 = (f32[1280,512]{1,0:T(8,128)}, f32[8,512]{1,0:T(8,128)}, f32[8,16,256]{2,1,0:T(8,128)}, f32[8,2,16,128]{3,2,1,0:T(8,128)}) custom-call(f32[5,8,32,512]{3,2,1,0:T(8,128)} %flow.1, f32[1280,512]{1,0:T(8,128)} %bitcast.5, f32[256,512]{1,0:T(8,128)} %bitcast.7, s32[1,192]{1,0:T(1,128)} %counts_h.1, s32[1,192]{1,0:T(1,128)} %bitcast.9, ...), custom_call_target="tpu_custom_call" | custom-call | tf_op jit(solution)/shard_map/train/pallas_call | solution.py:373
  70.7 3.7 %finish.1 = (f32[5,8,32,512]{3,2,1,0:T(8,128)}, f32[2,32,512]{2,1,0:T(8,128)}, f32[1]{0:T(128)}, f32[12,2048]{1,0:T(8,128)}, f32[16,2048]{1,0:T(8,128)}) custom-call(f32[5,8,32,512]{3,2,1,0:T(8,128)} %bitcast.6, f32[2,32,512]{2,1,0:T(8,128)} %stress_h.1, f32[8,512]{1,0:T(8,128)} %get-tuple-element.10.meta_h, f32[8,16,256]{2,1,0:T(8,128)} %get-tuple-element.11.small_h, ...), custom_call_target="tpu_custom_call" | custom-call | tf_op jit(solution)/shard_map/finish/pallas_call | solution.py:491
